TPU v7x, 256 devices: a whole 4x4x8 slice. The times are simulated.
256 devices in a mesh: tok: 32 (over x_lo, z, core), feat: 8 (over x_hi, y).
Axes of the slice: x: 4 (x_hi: 2, x_lo: 2; x = x_hi * 2 + x_lo), y: 4, z: 8, core: 2. Of those that a mesh axis runs over, the one named last changes fastest.
Arguments:
- teacher: bfloat16 [8192, 8192], P('tok', 'feat')
- student: bfloat16 [8192, 5120], P('tok', 'feat')
Outputs:
- loss: float32 [], replicated
- grad_student: float32 [8192, 5120], P('tok', 'feat')
All inputs are finite; a program needn't handle non-finite values.
Results may differ from a plain program's by a relative error of at most 0.0031.
Values may be sent and summed in bfloat16 or wider, within the bound.
A program may use at most 128 MiB of HBM per device.

v0:
```python
import jax
import jax.numpy as jnp
from jax import lax
from jax.sharding import PartitionSpec as P

DS = 5120


def gram_tile(rows, mine):
    return lax.dot_general(rows, mine, (((1,), (1,)), ((), ())), preferred_element_type=jnp.float32)


def local(teacher, student):
    width = teacher.shape[0]
    all_teacher, all_student = (
        lax.all_gather(teacher, "tok", axis=0, tiled=True),
        lax.all_gather(student, "tok", axis=0, tiled=True),
    )
    parts = lax.psum_scatter(
        jnp.concatenate([gram_tile(all_teacher, teacher), gram_tile(all_student, student)], axis=1),
        "feat",
        scatter_dimension=0,
        tiled=True,
    )
    kern = parts[:, :width]
    lern = parts[:, width:]
    local_sums = (jnp.sum(kern * lern), jnp.sum(kern * kern), jnp.sum(lern * lern))
    cross, ksq, lsq = lax.psum((local_sums[0], local_sums[1], local_sums[2]), ("tok", "feat"))
    knorm = jnp.sqrt(ksq)
    lnorm = jnp.sqrt(lsq)
    loss = -cross / (knorm * lnorm)
    weights = (-kern / (knorm * lnorm) + cross * lern / (knorm * lnorm**3)).astype(jnp.bfloat16)
    full_weights = lax.all_gather(weights, "feat", axis=0, tiled=True)
    scale = 2.0 * all_student.shape[0] * DS
    grad_student = scale * lax.dot_general(
        full_weights, all_student, (((0,), (0,)), ((), ())), preferred_element_type=jnp.float32
    )
    return (loss, grad_student)


def solution(mesh):
    placed = (P("tok", "feat"), P("tok", "feat"))
    return jax.shard_map(
        local, mesh=mesh, in_specs=placed, out_specs=(P(), P("tok", "feat")), check_vma=False
    )
```

profile of v0, /device:TPU:1, one launch (start us, length us, event | category | flops | bytes accessed | tf_op | source)
XLA Modules:
  0.0 575.2 jit_solution(16910604198474393018)
XLA Ops:
  7.2 0.0 all-gather.6.cloned.1.call-start
  7.2 0.7 all-gather.6.cloned.1.call-update
  7.9 0.0 all-gather.4.cloned.1.call-start
  7.9 0.7 all-gather.4.cloned.1.call-update
  8.6 0.0 copy-start.1
  8.7 0.0 reduce-scatter.2.cloned.1.call-start
  8.7 80.1 %all-gather.6.cloned.1.call-done = bf16[8192,640]{1,0:T(8,128)(2,1)} async-done(((bf16[256,640]{1,0:T(8,128)(2,1)}), bf16[8192,640]{1,0:T(8,128)(2,1)}) %all-gather.6.cloned.1.call-update) | async-done | bytes 10485776 | tf_op jit(solution)/shard_map/all_gather | solution.py:17
  88.8 10.7 %fusion.1 = f32[8192,256]{0,1:T(8,128)} fusion(bf16[8192,640]{1,0:T(8,128)(2,1)} %all-gather.6.cloned.1.call-done, bf16[256,640]{1,0:T(8,128)(2,1)} %param.3), kind=kOutput, calls=%fused_computation.7 | convolution fusion | flops 2684354560 | bytes 19202048 | tf_op jit(solution)/shard_map/dot_general | solution.py:10
  99.5 90.2 %all-gather.4.cloned.1.call-done = bf16[8192,1024]{1,0:T(8,128)(2,1)} async-done(((bf16[256,1024]{1,0:T(8,128)(2,1)}), bf16[8192,1024]{1,0:T(8,128)(2,1)}) %all-gather.4.cloned.1.call-update) | async-done | bytes 16777232 | tf_op jit(solution)/shard_map/all_gather | solution.py:16
  189.8 0.0 copy-done.1
  189.8 0.0 copy-start
  189.8 8.3 %fusion = f32[8192,256]{0,1:T(8,128)S(1)} fusion(bf16[8192,1024]{1,0:T(8,128)(2,1)} %all-gather.4.cloned.1.call-done, bf16[256,1024]{1,0:T(8,128)(2,1)S(1)} %copy-done.1), kind=kOutput, calls=%fused_computation.6 | convolution fusion | flops 4294967296 | bytes 25690112 | tf_op jit(solution)/shard_map/dot_general | solution.py:10
  198.1 0.0 copy-done
  198.1 6.2 %pad_maximum_fusion = f32[8192,512]{0,1:T(8,128)} fusion(f32[8192,256]{0,1:T(8,128)S(1)} %copy-done, f32[8192,256]{0,1:T(8,128)S(1)} %fusion), kind=kLoop, calls=%fused_computation | loop fusion | flops 4194304 | bytes 33554432 | tf_op jit(solution)/shard_map/concatenate | solution.py:20
  204.3 0.0 reduce-scatter.2.cloned.1.call-update
  204.3 0.0 all-gather.8.cloned.1.call-start
  204.4 195.3 %reduce-scatter.2.cloned.1.call-done = f32[1024,512]{0,1:T(8,128)} async-done(((f32[8192,512]{0,1:T(8,128)}), f32[1024,512]{0,1:T(8,128)}) %reduce-scatter.2.cloned.1.call-update) | async-done | bytes 2097168 | tf_op jit(solution)/shard_map/reduce_scatter | solution.py:19
  399.7 2.4 multiply_reduce_fusion
  402.1 78.7 %all-reduce = (f32[]{:T(128)}, f32[]{:T(128)}, f32[]{:T(128)}) all-reduce(f32[]{:T(128)} %get-tuple-element.3, f32[]{:T(128)} %get-tuple-element.4, f32[]{:T(128)} %get-tuple-element.2), channel_id=1, replica_groups=mesh['tok'=32,'feat'=8] {'tok','feat'}, use_global_device_ids=true, to_apply=%region_2.0 | all-reduce | flops 3 | bytes 24 | tf_op jit(solution)/shard_map/psum | solution.py:28
  482.2 3.3 add_convert_fusion
  485.5 0.0 all-gather.8.cloned.1.call-update
  486.3 71.7 %all-gather.8.cloned.1.call-done = bf16[8192,256]{0,1:T(8,128)(2,1)} async-done(((bf16[1024,256]{0,1:T(8,128)(2,1)}), bf16[8192,256]{0,1:T(8,128)(2,1)}) %all-gather.8.cloned.1.call-update) | async-done | bytes 4194320 | tf_op jit(solution)/shard_map/all_gather | solution.py:33
  558.0 9.5 %convolution_multiply_fusion = f32[256,640]{1,0:T(8,128)} fusion(bf16[8192,256]{0,1:T(8,128)(2,1)} %all-gather.8.cloned.1.call-done, bf16[8192,640]{1,0:T(8,128)(2,1)} %all-gather.6.cloned.1.call-done), kind=kOutput, calls=%fused_computation.1 | convolution fusion | flops 2684518400 | bytes 15335424 | tf_op jit(solution)/shard_map/dot_general | solution.py:35
Async XLA Ops:
  7.2 81.7 %all-gather.6.cloned.1.call-start = ((), (), s32[]{:S(2)}) async-start(), calls=%async_computation.2 | async-start | bytes 10813440 | tf_op jit(solution)/shard_map/all_gather | solution.py:17
  7.9 181.9 %all-gather.4.cloned.1.call-start = ((), (), s32[]{:S(2)}) async-start(), calls=%async_computation.1 | async-start | bytes 17301504 | tf_op jit(solution)/shard_map/all_gather | solution.py:16
  8.6 181.1 %copy-start.1 = (bf16[256,1024]{1,0:T(8,128)(2,1)S(1)}, bf16[256,1024]{1,0:T(8,128)(2,1)}, u32[]{:S(2)}) copy-start(bf16[256,1024]{1,0:T(8,128)(2,1)} %param.2) | copy-start | bytes 1572868
  8.7 391.0 %reduce-scatter.2.cloned.1.call-start = ((), (), s32[]{:S(2)}) async-start(), calls=%async_computation.3 | async-start | bytes 18874368 | tf_op jit(solution)/shard_map/reduce_scatter | solution.py:19
  189.8 8.3 %copy-start = (f32[8192,256]{0,1:T(8,128)S(1)}, f32[8192,256]{0,1:T(8,128)}, u32[]{:S(2)}) copy-start(f32[8192,256]{0,1:T(8,128)} %fusion.1) | copy-start | bytes 25165828
  204.3 353.6 %all-gather.8.cloned.1.call-start = ((), (), s32[]{:S(2)}) async-start(), calls=%async_computation.4 | async-start | bytes 4718592 | tf_op jit(solution)/shard_map/all_gather | solution.py:33
Sparse Core Ops, SparseCore 0:
  9.9 78.9 all-gather.5
  90.7 99.0 all-gather.3
  204.5 195.1 reduce-scatter.1
  485.6 72.2 all-gather.7
where the time goes:
time: 575 us
  waiting for transfers between devices  439 us (76%)
  blocking collectives  78.7 us (14%)
  matrix products  28.5 us (5%)
  between operations  17 us (3%)
  other arithmetic  11.9 us (2%)
    reduce_scatter x1, waiting for transfers between devices, local(): lax.psum_scatter(jnp.concatenate([gram_tile(all_teacher, teacher), gram_t...  195 us
    all_gather x1, waiting for transfers between devices, local(): lax.all_gather(teacher, 'tok', axis=0, tiled=True)  90.2 us
    all_gather x1, waiting for transfers between devices, local(): lax.all_gather(student, 'tok', axis=0, tiled=True)  80.1 us
    psum x1, blocking collectives, local(): lax.psum((local_sums[0], local_sums[1], local_sums[2]), ('tok', 'feat'))  78.7 us
    all_gather x1, waiting for transfers between devices, local(): full_weights = lax.all_gather(weights, 'feat', axis=0, tiled=True)  71.7 us
    dot_general x2, matrix products, gram_tile(): lax.dot_general(rows, mine, (((1,), (1,)), ((), ())), preferred_element_t...  19 us
  transfers between devices with their start and end apart: 4, of which 4 were waited for; matrix products, arithmetic and copies ran while one was open for 2% of the time, Pallas kernels for 0%

commit v1 on v0

v1 whole, which is shorter than its diff:
```python
import functools

import jax
import jax.numpy as jnp
from jax import lax
from jax.experimental import pallas as pl
from jax.experimental.pallas import tpu as pltpu
from jax.sharding import PartitionSpec as P

TOKENS = 8192
DS = 5120
MESH = pl.DeviceIdType.MESH
F32 = jnp.float32
BF16 = jnp.bfloat16


def slot(k):
    return k if k <= 4 else 12 - k


def kernel(
    t_ref, s_ref, loss_ref, grad_ref,
    tb, sb, stage, rs, own, total, wn, wt, tst, red, redr, acc,
    t_ring, t_core, t_ring_out, t_core_out,
    s_ring, s_core, s_ring_out, s_core_out, x_out,
    rs_in, rs_out, red_in, red_out, tr_in, tr_out, agn_in, agn_out, agt_in, agt_out,
):
    tok = lax.axis_index("tok")
    feat = lax.axis_index("feat")
    core = lax.rem(tok, 2)
    z = lax.rem(tok // 2, 8)
    xl = tok // 16
    y = lax.rem(feat, 4)
    xh = feat // 4

    def tok_of(x_lo, zz, c):
        return (x_lo * 8 + lax.rem(zz + 16, 8)) * 2 + c

    z_down = (tok_of(xl, z - 1, core), feat)
    z_up = (tok_of(xl, z + 1, core), feat)
    x_other = (tok_of(1 - xl, z, core), feat)
    sibling = (tok_of(xl, z, 1 - core), feat)

    def feat_peer(p):
        return lax.rem(feat + p, 8)

    swapped = core * 4 + y

    barrier = pltpu.get_barrier_semaphore()

    def greet(device):
        pl.semaphore_signal(barrier, inc=1, device_id=device, device_id_type=MESH)

    for p in range(1, 8):
        greet((tok, feat_peer(p)))
        greet((tok_of(xl, z + p, core), feat))
    for device in (x_other, sibling, (tok_of(1 - xl, z, 1 - core), feat)):
        greet(device)
    for s in (1, 2, 3):
        for sign in (s, -s):
            greet((tok_of(xl, z + sign, xh), swapped))
            greet((tok_of(1 - xl, z + sign, xh), swapped))
    pl.semaphore_wait(barrier, 29)

    def send(src, dst, out_sem, in_sem, device):
        pltpu.make_async_remote_copy(
            src_ref=src, dst_ref=dst, send_sem=out_sem, recv_sem=in_sem, device_id=device, device_id_type=MESH
        ).start()

    def wait(ref, sem):
        pltpu.make_async_copy(ref, ref, sem).wait()

    T = (t_ref, tb, t_ring, t_core, t_ring_out, t_core_out, 4)
    S = (s_ref, sb, s_ring, s_core, s_ring_out, s_core_out, 7)

    def launch(kind, index):
        src, buf, ring, cores, ring_out, core_out, last = kind
        for h in range(2):
            a = 2 * core + h
            rows = src.at[h * 128 : (h + 1) * 128]
            send(rows, buf.at[a, 0, 1], x_out.at[index], ring.at[0, 1, h], x_other)
            send(rows, buf.at[a, 1, 0], ring_out.at[0], ring.at[1, 0, h], z_down)
        for h in range(2):
            a = 2 * core + h
            rows = src.at[h * 128 : (h + 1) * 128]
            send(rows, buf.at[a, 0, 0], core_out.at[0], cores.at[0], sibling)
            buf[a, 0, 0] = src[h * 128 : (h + 1) * 128]

    def relay(kind, k):
        src, buf, ring, cores, ring_out, core_out, last = kind
        here, there = slot(k), slot(k + 1)
        for h in range(2):
            a = 2 * core + h
            for side in (0, 1) if k else (1,):
                block = buf.at[a, here, side]
                wait(block, ring.at[here, side, h])
                if k < last:
                    to = z_up if side else z_down
                    send(block, buf.at[a, there, side], ring_out.at[k], ring.at[there, side, h], to)
                send(block, block, core_out.at[here], cores.at[here], sibling)

    def have(kind, k):
        wait(kind[1].at[0:2, slot(k)], kind[3].at[slot(k)])

    def partials(kind, s, j):
        src, buf = kind[0], kind[1]

        @pl.loop(0, 4)
        def _(p):
            a = lax.rem(feat // 2 + p, 4)
            rows = buf[a, s].reshape(256, src.shape[1])
            x = lax.dot_general(src[...], rows, (((1,), (1,)), ((), ())), preferred_element_type=F32)
            for b in range(2):
                f = 2 * a + b
                tile = x[b * 128 : (b + 1) * 128]

                @pl.when(f == feat)
                def _():
                    own[j] = tile

                @pl.when(f != feat)
                def _():
                    stage[j, f] = tile.astype(BF16)
                    send(stage.at[j, f], rs.at[j, feat], rs_out.at[j], rs_in.at[j], (tok, f))

    def add_up(j):
        wait(rs.at[j, 0:7], rs_in.at[j])
        total[j] = own[j]

        @pl.loop(1, 8)
        def _(p):
            total[j] += rs[j, feat_peer(p)].astype(F32)

    def fold(v):
        v = jnp.sum(v.reshape(16, 8, 256), axis=0)
        return v[:, :128] + v[:, 128:]

    def norms(s):
        k, l = total[s], total[5 + s]
        weight = 2.0 if s in (1, 2, 3) else 1.0
        for i, v in enumerate((k * l, k * k, l * l)):
            v = weight * fold(v)
            if s:
                red[0, i] += v
            else:
                red[0, i] = v

    launch(T, 0)
    launch(S, 1)
    for s in range(5):
        relay(T, s)
        have(T, s)
        partials(T, s, s)
        relay(S, s)
        have(S, s)
        partials(S, s, 5 + s)
        if s:
            add_up(s - 1)
            add_up(5 + s - 1)
            norms(s - 1)
    add_up(4)
    add_up(9)
    norms(4)

    groups = (
        [(tok, feat_peer(p)) for p in range(1, 8)],
        [(tok_of(xl, z + p, core), feat) for p in range(1, 8)],
        [x_other, sibling, (tok_of(1 - xl, z, 1 - core), feat)],
    )
    for g, peers in enumerate(groups):
        n = len(peers)
        for i, device in enumerate(peers):
            send(red.at[g], redr.at[g, i], red_out.at[g], red_in.at[g], device)
        wait(redr.at[g, 0:n], red_in.at[g])
        v = red[g]
        for i in range(n):
            v = v + redr[g, i]
        red[g + 1] = v

    cross = jnp.sum(red[3, 0], axis=(0, 1), keepdims=True)
    knorm = jnp.sqrt(jnp.sum(red[3, 1], axis=(0, 1), keepdims=True))
    lnorm = jnp.sqrt(jnp.sum(red[3, 2], axis=(0, 1), keepdims=True))
    loss_ref[...] = -cross / (knorm * lnorm)
    by_kern = -1.0 / (knorm * lnorm)
    by_lern = cross / (knorm * lnorm * lnorm * lnorm)

    def weights(s):
        return by_kern * total[s] + by_lern * total[5 + s]

    for s in (1, 2, 3):
        w = weights(s)
        wn[feat, :, s * 256 : (s + 1) * 256] = w.astype(BF16)
        theirs = (core * 2 + lax.rem(y, 2)) * 2 + y // 2
        for side in range(2):
            i = 2 * (s - 1) + side
            tst[i] = jnp.transpose(w[:, side * 128 : (side + 1) * 128]).astype(BF16)
            to = (tok_of(1 - xl, z - s, xh), swapped) if side else (tok_of(xl, z + s, xh), swapped)
            send(tst.at[i], wt.at[theirs, :, i * 128 : (i + 1) * 128], tr_out.at[0], tr_in.at[0], to)
    for s in (0, 4):
        wn[feat, :, s * 256 : (s + 1) * 256] = weights(s).astype(BF16)
    for p in range(1, 8):
        send(wn.at[feat], wn.at[feat], agn_out.at[0], agn_in.at[feat], (tok, feat_peer(p)))
    relay(S, 5)

    def mine_t(f):
        return ((f // 4) * 2 + lax.rem(f, 2)) * 2 + lax.rem(f, 4) // 2

    me_t = mine_t(feat)
    wait(wt.at[me_t], tr_in.at[0])
    for p in range(1, 8):
        send(wt.at[me_t], wt.at[me_t], agt_out.at[0], agt_in.at[me_t], (tok, feat_peer(p)))
    relay(S, 6)
    relay(S, 7)

    acc[...] = jnp.zeros_like(acc)

    def pair(buf, sem, mine, a):
        for b in range(2):
            f = 2 * a + b

            @pl.when(f != mine)
            def _():
                wait(buf.at[f], sem.at[f])

    @pl.loop(0, 4)
    def _(p):
        a = lax.rem(feat // 2 + p, 4)
        pair(wn, agn_in, feat, a)
        w = wn[pl.ds(2 * a, 2)].reshape(256, 1280)
        acc[...] += jnp.dot(w, sb[a, 0:5].reshape(1280, 640), preferred_element_type=F32)

    for k in (5, 6, 7):
        have(S, k)

    @pl.loop(0, 4)
    def _(p):
        a = lax.rem(me_t // 2 + p, 4)
        pair(wt, agt_in, me_t, a)
        w = wt[pl.ds(2 * a, 2)].reshape(256, 768)
        acc[...] += jnp.dot(w, sb[a, 5:8].reshape(768, 640), preferred_element_type=F32)

    grad_ref[...] = (2.0 * TOKENS * DS) * acc[...]

    for kind, index in ((T, 0), (S, 1)):
        src, buf, ring, cores, ring_out, core_out, last = kind
        wait(src, x_out.at[index])
        for k in range(last):
            wait(buf.at[0:2, 0] if k else buf.at[0:2, 0], ring_out.at[k])
        for k in range(last + 1):
            wait(buf.at[0:2, 0], core_out.at[k])
    for j in range(10):
        wait(rs.at[j, 0:7], rs_out.at[j])
    for g, peers in enumerate(groups):
        wait(redr.at[g, 0 : len(peers)], red_out.at[g])
    wait(wt.at[0], tr_out.at[0])
    wait(wn.at[0:7], agn_out.at[0])
    wait(wt.at[0:7], agt_out.at[0])


def local(teacher, student):
    rows, dt = teacher.shape
    ds = student.shape[1]
    dma = pltpu.SemaphoreType.DMA
    loss, grad = pl.pallas_call(
        kernel,
        out_shape=(jax.ShapeDtypeStruct((1, 1), F32), jax.ShapeDtypeStruct((rows, ds), F32)),
        in_specs=[pl.BlockSpec(memory_space=pltpu.VMEM)] * 2,
        out_specs=[pl.BlockSpec(memory_space=pltpu.VMEM)] * 2,
        scratch_shapes=[
            pltpu.VMEM((4, 5, 2, 128, dt), BF16),
            pltpu.VMEM((4, 8, 2, 128, ds), BF16),
            pltpu.VMEM((10, 8, 128, 256), BF16),
            pltpu.VMEM((10, 8, 128, 256), BF16),
            pltpu.VMEM((10, 128, 256), F32),
            pltpu.VMEM((10, 128, 256), F32),
            pltpu.VMEM((8, 128, 1280), BF16),
            pltpu.VMEM((8, 128, 768), BF16),
            pltpu.VMEM((6, 128, 128), BF16),
            pltpu.VMEM((4, 3, 8, 128), F32),
            pltpu.VMEM((3, 7, 3, 8, 128), F32),
            pltpu.VMEM((rows, ds), F32),
            dma((5, 2, 2)), dma((5,)), dma((4,)), dma((5,)),
            dma((8, 2, 2)), dma((8,)), dma((7,)), dma((8,)), dma((2,)),
            dma((10,)), dma((10,)), dma((3,)), dma((3,)), dma((1,)), dma((1,)),
            dma((8,)), dma((1,)), dma((8,)), dma((1,)),
        ],
        compiler_params=pltpu.CompilerParams(
            collective_id=0, has_side_effects=True, vmem_limit_bytes=60 * 2**20
        ),
        cost_estimate=pl.CostEstimate(flops=7 * 10**9, bytes_accessed=2 * 10**6, transcendentals=0),
    )(teacher, student)
    return loss.reshape(()), grad


def solution(mesh):
    placed = (P("tok", "feat"), P("tok", "feat"))
    return jax.shard_map(
        local, mesh=mesh, in_specs=placed, out_specs=(P(), P("tok", "feat")), check_vma=False
    )
```

time: 575 us -> 189 us (0.33)
  the two profiles are of different devices: /device:TPU:1 before, /device:TPU:26 now
where the time goes in v1:
time: 189 us
  Pallas kernels  185 us (98%)
  between operations  2.39 us (1%)
  local copies, waits for them, and re-layouts  1.97 us (1%)
    pallas_call x1, Pallas kernels, local(): pl.pallas_call(kernel, out_shape=(jax.ShapeDtypeStruct((1, 1), F32), jax....  185 us

profile of v1, /device:TPU:26, one launch (start us, length us, event | category | flops | bytes accessed | tf_op | source)
XLA Modules:
  0.0 189.2 jit_solution(6810931359765933680)
XLA Ops:
  0.6 184.8 %shard_map.41 = (f32[1,1]{1,0:T(1,128)}, f32[256,640]{1,0:T(8,128)}) custom-call(bf16[256,1024]{1,0:T(8,128)(2,1)} %t_ref.1, bf16[256,640]{1,0:T(8,128)(2,1)} %s_ref.1), custom_call_target="tpu_custom_call" | custom-call | flops 7000000000 | bytes 2000000 | tf_op jit(solution)/shard_map/pallas_call | solution.py:264
  186.1 2.0 %copy.7 = f32[256,640]{1,0:T(8,128)} copy(f32[256,640]{1,0:T(8,128)} %get-tuple-element.9) | data formatting | bytes 1310720

commit v2 on v1

--- a/solution.py
+++ b/solution.py
@@ -83,35 +83,39 @@
         for h in range(2):
             a = 2 * core + h
             rows = src.at[h * 128 : (h + 1) * 128]
-            send(rows, buf.at[a, 0, 0], core_out.at[0], cores.at[0], sibling)
+            send(rows, buf.at[a, 0, 0], core_out.at[0], cores.at[0, h], sibling)
             buf[a, 0, 0] = src[h * 128 : (h + 1) * 128]
 
-    def relay(kind, k):
+    def relay(kind, k, h):
         src, buf, ring, cores, ring_out, core_out, last = kind
         here, there = slot(k), slot(k + 1)
-        for h in range(2):
-            a = 2 * core + h
-            for side in (0, 1) if k else (1,):
-                block = buf.at[a, here, side]
-                wait(block, ring.at[here, side, h])
-                if k < last:
-                    to = z_up if side else z_down
-                    send(block, buf.at[a, there, side], ring_out.at[k], ring.at[there, side, h], to)
-                send(block, block, core_out.at[here], cores.at[here], sibling)
-
-    def have(kind, k):
-        wait(kind[1].at[0:2, slot(k)], kind[3].at[slot(k)])
-
-    def partials(kind, s, j):
+        a = 2 * core + h
+        for side in (0, 1) if k else (1,):
+            block = buf.at[a, here, side]
+            wait(block, ring.at[here, side, h])
+            if k < last:
+                to = z_up if side else z_down
+                send(block, buf.at[a, there, side], ring_out.at[k], ring.at[there, side, h], to)
+            send(block, block, core_out.at[here], cores.at[here, h], sibling)
+
+    def have(kind, k, h):
+        wait(kind[1].at[0, slot(k)], kind[3].at[slot(k), h])
+
+    def partials(kind, s, j, h):
         src, buf = kind[0], kind[1]
 
-        @pl.loop(0, 4)
+        @pl.loop(0, 2)
         def _(p):
-            a = lax.rem(feat // 2 + p, 4)
+            a = 2 * lax.rem(core + p, 2) + h
+
+            @pl.when(p == 1)
+            def _():
+                have(kind, s, h)
+
             rows = buf[a, s].reshape(256, src.shape[1])
             x = lax.dot_general(src[...], rows, (((1,), (1,)), ((), ())), preferred_element_type=F32)
             for b in range(2):
-                f = 2 * a + b
+                f = (a // 2) * 4 + lax.rem(a, 2) + 2 * b
                 tile = x[b * 128 : (b + 1) * 128]
 
                 @pl.when(f == feat)
@@ -145,15 +149,13 @@
             else:
                 red[0, i] = v
 
-    launch(T, 0)
-    launch(S, 1)
+    launch(S, 0)
+    launch(T, 1)
     for s in range(5):
-        relay(T, s)
-        have(T, s)
-        partials(T, s, s)
-        relay(S, s)
-        have(S, s)
-        partials(S, s, 5 + s)
+        for kind, j in ((S, 5 + s), (T, s)):
+            for h in range(2):
+                relay(kind, s, h)
+                partials(kind, s, j, h)
         if s:
             add_up(s - 1)
             add_up(5 + s - 1)
@@ -187,65 +189,109 @@
     def weights(s):
         return by_kern * total[s] + by_lern * total[5 + s]
 
+    def tile_of(f):
+        return ((f // 4) * 2 + lax.rem(f, 2)) * 2 + lax.rem(f, 4) // 2
+
+    here = tile_of(feat)
     for s in (1, 2, 3):
         w = weights(s)
-        wn[feat, :, s * 256 : (s + 1) * 256] = w.astype(BF16)
-        theirs = (core * 2 + lax.rem(y, 2)) * 2 + y // 2
+        wn[here, :, s * 256 : (s + 1) * 256] = w.astype(BF16)
         for side in range(2):
             i = 2 * (s - 1) + side
             tst[i] = jnp.transpose(w[:, side * 128 : (side + 1) * 128]).astype(BF16)
             to = (tok_of(1 - xl, z - s, xh), swapped) if side else (tok_of(xl, z + s, xh), swapped)
-            send(tst.at[i], wt.at[theirs, :, i * 128 : (i + 1) * 128], tr_out.at[0], tr_in.at[0], to)
+            send(tst.at[i], wt.at[swapped, :, i * 128 : (i + 1) * 128], tr_out.at[0], tr_in.at[0], to)
     for s in (0, 4):
-        wn[feat, :, s * 256 : (s + 1) * 256] = weights(s).astype(BF16)
-    for p in range(1, 8):
-        send(wn.at[feat], wn.at[feat], agn_out.at[0], agn_in.at[feat], (tok, feat_peer(p)))
-    relay(S, 5)
-
-    def mine_t(f):
-        return ((f // 4) * 2 + lax.rem(f, 2)) * 2 + lax.rem(f, 4) // 2
-
-    me_t = mine_t(feat)
-    wait(wt.at[me_t], tr_in.at[0])
-    for p in range(1, 8):
-        send(wt.at[me_t], wt.at[me_t], agt_out.at[0], agt_in.at[me_t], (tok, feat_peer(p)))
-    relay(S, 6)
-    relay(S, 7)
-
+        wn[here, :, s * 256 : (s + 1) * 256] = weights(s).astype(BF16)
+
+    up = xh * 4 + lax.rem(y + 1, 4)
+    down = xh * 4 + lax.rem(y + 3, 4)
+    far = xh * 4 + lax.rem(y + 2, 4)
+
+    def across(f):
+        return lax.rem(f + 4, 8)
+
+    N = (wn, tile_of, agn_out, agn_in)
+    R = (wt, lambda f: f, agt_out, agt_in)
+
+    def give(group, f, part, to, i):
+        buf, place, out, into = group
+        ref = buf.at[place(f)]
+        if part is not None:
+            ref = ref.at[part * 64 : (part + 1) * 64]
+        send(ref, ref, out.at[0], into.at[i], (tok, to))
+
+    def got(group, f, part, i):
+        buf, place, out, into = group
+        ref = buf.at[place(f)]
+        if part is not None:
+            ref = ref.at[part * 64 : (part + 1) * 64]
+        wait(ref, into.at[i])
+
+    def first(group):
+        give(group, feat, None, up, 0)
+        give(group, feat, None, down, 1)
+        give(group, feat, None, across(feat), 2)
+
+    def second(group):
+        got(group, down, None, 0)
+        give(group, down, 0, up, 3)
+        got(group, up, None, 1)
+        give(group, up, 1, down, 4)
+        got(group, across(feat), None, 2)
+        give(group, across(feat), None, up, 5)
+        give(group, across(feat), None, down, 6)
+
+    def third(group):
+        for part in range(2):
+            got(group, far, part, 3 + part)
+            give(group, far, part, across(feat), 7 + part)
+
+    def fourth(group):
+        got(group, across(down), None, 5)
+        got(group, across(up), None, 6)
+        for part in range(2):
+            got(group, across(far), part, 7 + part)
+
+    def product(buf, plane, lo, hi):
+        @pl.loop(0, 2)
+        def _(p):
+            a = 2 * plane + p
+            depth = (hi - lo) * 256
+            w = buf[pl.ds(2 * a, 2)].reshape(256, depth)
+            acc[...] += jnp.dot(w, sb[a, lo:hi].reshape(depth, DS // 8), preferred_element_type=F32)
+
+    first(N)
+    for h in range(2):
+        relay(S, 5, h)
+    wait(wt.at[feat], tr_in.at[0])
+    first(R)
+    second(N)
+    for h in range(2):
+        relay(S, 6, h)
+    second(R)
+    third(N)
+    for h in range(2):
+        relay(S, 7, h)
+    third(R)
     acc[...] = jnp.zeros_like(acc)
-
-    def pair(buf, sem, mine, a):
-        for b in range(2):
-            f = 2 * a + b
-
-            @pl.when(f != mine)
-            def _():
-                wait(buf.at[f], sem.at[f])
-
-    @pl.loop(0, 4)
-    def _(p):
-        a = lax.rem(feat // 2 + p, 4)
-        pair(wn, agn_in, feat, a)
-        w = wn[pl.ds(2 * a, 2)].reshape(256, 1280)
-        acc[...] += jnp.dot(w, sb[a, 0:5].reshape(1280, 640), preferred_element_type=F32)
-
+    product(wn, xh, 0, 5)
     for k in (5, 6, 7):
-        have(S, k)
-
-    @pl.loop(0, 4)
-    def _(p):
-        a = lax.rem(me_t // 2 + p, 4)
-        pair(wt, agt_in, me_t, a)
-        w = wt[pl.ds(2 * a, 2)].reshape(256, 768)
-        acc[...] += jnp.dot(w, sb[a, 5:8].reshape(768, 640), preferred_element_type=F32)
+        for h in range(2):
+            have(S, k, h)
+    product(wt, xh, 5, 8)
+    fourth(N)
+    product(wn, 1 - xh, 0, 5)
+    fourth(R)
+    product(wt, 1 - xh, 5, 8)
 
     grad_ref[...] = (2.0 * TOKENS * DS) * acc[...]
 
-    for kind, index in ((T, 0), (S, 1)):
+    for kind, index in ((S, 0), (T, 1)):
         src, buf, ring, cores, ring_out, core_out, last = kind
         wait(src, x_out.at[index])
         for k in range(last):
-            wait(buf.at[0:2, 0] if k else buf.at[0:2, 0], ring_out.at[k])
+            wait(buf.at[0:2, 0], ring_out.at[k])
         for k in range(last + 1):
             wait(buf.at[0:2, 0], core_out.at[k])
     for j in range(10):
@@ -279,10 +325,10 @@
             pltpu.VMEM((4, 3, 8, 128), F32),
             pltpu.VMEM((3, 7, 3, 8, 128), F32),
             pltpu.VMEM((rows, ds), F32),
-            dma((5, 2, 2)), dma((5,)), dma((4,)), dma((5,)),
-            dma((8, 2, 2)), dma((8,)), dma((7,)), dma((8,)), dma((2,)),
+            dma((5, 2, 2)), dma((5, 2)), dma((4,)), dma((5,)),
+            dma((8, 2, 2)), dma((8, 2)), dma((7,)), dma((8,)), dma((2,)),
             dma((10,)), dma((10,)), dma((3,)), dma((3,)), dma((1,)), dma((1,)),
-            dma((8,)), dma((1,)), dma((8,)), dma((1,)),
+            dma((9,)), dma((1,)), dma((9,)), dma((1,)),
         ],
         compiler_params=pltpu.CompilerParams(
             collective_id=0, has_side_effects=True, vmem_limit_bytes=60 * 2**20

time: 189 us -> 157 us (0.83)
  the two profiles are of different devices: /device:TPU:26 before, /device:TPU:1 now
where the time goes in v2:
time: 157 us
  Pallas kernels  152 us (97%)
  between operations  2.39 us (2%)
  local copies, waits for them, and re-layouts  1.97 us (1%)
    pallas_call x1, Pallas kernels, local(): pl.pallas_call(kernel, out_shape=(jax.ShapeDtypeStruct((1, 1), F32), jax....  152 us

profile of v2, /device:TPU:1, one launch (start us, length us, event | category | flops | bytes accessed | tf_op | source)
XLA Modules:
  0.0 156.8 jit_solution(1222942214906558621)
XLA Ops:
  0.6 152.4 %shard_map.41 = (f32[1,1]{1,0:T(1,128)}, f32[256,640]{1,0:T(8,128)}) custom-call(bf16[256,1024]{1,0:T(8,128)(2,1)} %t_ref.1, bf16[256,640]{1,0:T(8,128)(2,1)} %s_ref.1), custom_call_target="tpu_custom_call" | custom-call | flops 7000000000 | bytes 2000000 | tf_op jit(solution)/shard_map/pallas_call | solution.py:310
  153.7 2.0 %copy.7 = f32[256,640]{1,0:T(8,128)} copy(f32[256,640]{1,0:T(8,128)} %get-tuple-element.9) | data formatting | bytes 1310720

commit v3 on v2

--- a/solution.py
+++ b/solution.py
@@ -53,14 +53,9 @@
 
     for p in range(1, 8):
         greet((tok, feat_peer(p)))
-        greet((tok_of(xl, z + p, core), feat))
-    for device in (x_other, sibling, (tok_of(1 - xl, z, 1 - core), feat)):
+    for device in (z_down, z_up, x_other, sibling):
         greet(device)
-    for s in (1, 2, 3):
-        for sign in (s, -s):
-            greet((tok_of(xl, z + sign, xh), swapped))
-            greet((tok_of(1 - xl, z + sign, xh), swapped))
-    pl.semaphore_wait(barrier, 29)
+    pl.semaphore_wait(barrier, 11)
 
     def send(src, dst, out_sem, in_sem, device):
         pltpu.make_async_remote_copy(
@@ -86,17 +81,26 @@
             send(rows, buf.at[a, 0, 0], core_out.at[0], cores.at[0, h], sibling)
             buf[a, 0, 0] = src[h * 128 : (h + 1) * 128]
 
-    def relay(kind, k, h):
+    def relay(kind, k, h, sides=(0, 1)):
         src, buf, ring, cores, ring_out, core_out, last = kind
         here, there = slot(k), slot(k + 1)
         a = 2 * core + h
-        for side in (0, 1) if k else (1,):
+        for side in sides if k else (1,):
             block = buf.at[a, here, side]
             wait(block, ring.at[here, side, h])
-            if k < last:
+            send(block, block, core_out.at[here], cores.at[here, h], sibling)
+            if k < last and k != 4:
                 to = z_up if side else z_down
                 send(block, buf.at[a, there, side], ring_out.at[k], ring.at[there, side, h], to)
-            send(block, block, core_out.at[here], cores.at[here, h], sibling)
+
+    def pass_on(kind, k):
+        src, buf, ring, cores, ring_out, core_out, last = kind
+        here, there = slot(k), slot(k + 1)
+        for h in range(2):
+            for side in range(2):
+                a = 2 * core + h
+                to = z_up if side else z_down
+                send(buf.at[a, here, side], buf.at[a, there, side], ring_out.at[k], ring.at[there, side, h], to)
 
     def have(kind, k, h):
         wait(kind[1].at[0, slot(k)], kind[3].at[slot(k), h])
@@ -129,59 +133,65 @@
 
     def add_up(j):
         wait(rs.at[j, 0:7], rs_in.at[j])
-        total[j] = own[j]
-
-        @pl.loop(1, 8)
-        def _(p):
-            total[j] += rs[j, feat_peer(p)].astype(F32)
-
-    def fold(v):
-        v = jnp.sum(v.reshape(16, 8, 256), axis=0)
-        return v[:, :128] + v[:, 128:]
+
+        @pl.loop(0, 4)
+        def _(i):
+            rows = pl.ds(pl.multiple_of(i * 32, 32), 32)
+            v = own[j, rows]
+            for p in range(1, 8):
+                v = v + rs[j, feat_peer(p), rows].astype(F32)
+            total[j, rows] = v
 
     def norms(s):
         k, l = total[s], total[5 + s]
         weight = 2.0 if s in (1, 2, 3) else 1.0
         for i, v in enumerate((k * l, k * k, l * l)):
-            v = weight * fold(v)
-            if s:
-                red[0, i] += v
-            else:
-                red[0, i] = v
+            v = weight * jnp.sum(v, axis=0, keepdims=True)
+            red[0, i : i + 1] += v[:, :128] + v[:, 128:]
+
+    def step_sums(s):
+        add_up(5 + s)
+        add_up(s)
+        norms(s)
 
     launch(S, 0)
     launch(T, 1)
+    red[0] = jnp.zeros((8, 128), F32)
     for s in range(5):
         for kind, j in ((S, 5 + s), (T, s)):
+            early = False
+            for h in range(2) if early else ():
+                relay(kind, s, h, (0,))
             for h in range(2):
-                relay(kind, s, h)
+                relay(kind, s, h, (1,) if early else (0, 1))
+                if kind is T and s == 4 and h == 1:
+                    pass_on(S, 4)
                 partials(kind, s, j, h)
-        if s:
-            add_up(s - 1)
-            add_up(5 + s - 1)
-            norms(s - 1)
-    add_up(4)
-    add_up(9)
-    norms(4)
+            if kind is S and s:
+                step_sums(s - 1)
+    step_sums(4)
+
+    def tok_at(p, q):
+        return tok_of(lax.rem(xl + p, 2), z, core), feat_peer(q)
 
     groups = (
-        [(tok, feat_peer(p)) for p in range(1, 8)],
-        [(tok_of(xl, z + p, core), feat) for p in range(1, 8)],
-        [x_other, sibling, (tok_of(1 - xl, z, 1 - core), feat)],
+        [tok_at(p, q) for p in range(2) for q in range(8) if p or q],
+        [(tok_of(xl, z + p, lax.rem(core + q, 2)), feat) for q in range(2) for p in range(8) if p or q],
     )
     for g, peers in enumerate(groups):
-        n = len(peers)
         for i, device in enumerate(peers):
             send(red.at[g], redr.at[g, i], red_out.at[g], red_in.at[g], device)
-        wait(redr.at[g, 0:n], red_in.at[g])
+        for h in range(2):
+            relay(S, 5 + g, h)
+        wait(redr.at[g], red_in.at[g])
         v = red[g]
-        for i in range(n):
+        for i in range(15):
             v = v + redr[g, i]
         red[g + 1] = v
 
-    cross = jnp.sum(red[3, 0], axis=(0, 1), keepdims=True)
-    knorm = jnp.sqrt(jnp.sum(red[3, 1], axis=(0, 1), keepdims=True))
-    lnorm = jnp.sqrt(jnp.sum(red[3, 2], axis=(0, 1), keepdims=True))
+    cross, ksq, lsq = (jnp.sum(red[2, i : i + 1], axis=1, keepdims=True) for i in range(3))
+    knorm = jnp.sqrt(ksq)
+    lnorm = jnp.sqrt(lsq)
     loss_ref[...] = -cross / (knorm * lnorm)
     by_kern = -1.0 / (knorm * lnorm)
     by_lern = cross / (knorm * lnorm * lnorm * lnorm)
@@ -262,17 +272,13 @@
             acc[...] += jnp.dot(w, sb[a, lo:hi].reshape(depth, DS // 8), preferred_element_type=F32)
 
     first(N)
-    for h in range(2):
-        relay(S, 5, h)
     wait(wt.at[feat], tr_in.at[0])
     first(R)
     second(N)
     for h in range(2):
-        relay(S, 6, h)
+        relay(S, 7, h)
     second(R)
     third(N)
-    for h in range(2):
-        relay(S, 7, h)
     third(R)
     acc[...] = jnp.zeros_like(acc)
     product(wn, xh, 0, 5)
@@ -297,7 +303,7 @@
     for j in range(10):
         wait(rs.at[j, 0:7], rs_out.at[j])
     for g, peers in enumerate(groups):
-        wait(redr.at[g, 0 : len(peers)], red_out.at[g])
+        wait(redr.at[g], red_out.at[g])
     wait(wt.at[0], tr_out.at[0])
     wait(wn.at[0:7], agn_out.at[0])
     wait(wt.at[0:7], agt_out.at[0])
@@ -322,12 +328,12 @@
             pltpu.VMEM((8, 128, 1280), BF16),
             pltpu.VMEM((8, 128, 768), BF16),
             pltpu.VMEM((6, 128, 128), BF16),
-            pltpu.VMEM((4, 3, 8, 128), F32),
-            pltpu.VMEM((3, 7, 3, 8, 128), F32),
+            pltpu.VMEM((3, 8, 128), F32),
+            pltpu.VMEM((2, 15, 8, 128), F32),
             pltpu.VMEM((rows, ds), F32),
             dma((5, 2, 2)), dma((5, 2)), dma((4,)), dma((5,)),
             dma((8, 2, 2)), dma((8, 2)), dma((7,)), dma((8,)), dma((2,)),
-            dma((10,)), dma((10,)), dma((3,)), dma((3,)), dma((1,)), dma((1,)),
+            dma((10,)), dma((10,)), dma((2,)), dma((2,)), dma((1,)), dma((1,)),
             dma((9,)), dma((1,)), dma((9,)), dma((1,)),
         ],
         compiler_params=pltpu.CompilerParams(

time: 157 us -> 157 us (level); the launches traced: 157 us -> 154 us
  Pallas kernels: 152 us -> 150 us
    pallas_call x1, Pallas kernels: 152 us -> 150 us  [local(): pl.pallas_call(kernel, out_shape=(jax.ShapeDtypeStruct((1, 1), F32), jax....]
where the time goes in v3:
time: 157 us; the launch traced here: 154 us
  Pallas kernels  150 us (96%)
  between operations  2.39 us (2%)
  local copies, waits for them, and re-layouts  1.97 us (1%)
    pallas_call x1, Pallas kernels, local(): pl.pallas_call(kernel, out_shape=(jax.ShapeDtypeStruct((1, 1), F32), jax....  150 us

profile of v3, /device:TPU:1, one launch (start us, length us, event | category | flops | bytes accessed | tf_op | source)
XLA Modules:
  0.0 154.2 jit_solution(18223973068130512010)
XLA Ops:
  0.6 149.8 %shard_map.41 = (f32[1,1]{1,0:T(1,128)}, f32[256,640]{1,0:T(8,128)}) custom-call(bf16[256,1024]{1,0:T(8,128)(2,1)} %t_ref.1, bf16[256,640]{1,0:T(8,128)(2,1)} %s_ref.1), custom_call_target="tpu_custom_call" | custom-call | flops 7000000000 | bytes 2000000 | tf_op jit(solution)/shard_map/pallas_call | solution.py:316
  151.1 2.0 %copy.7 = f32[256,640]{1,0:T(8,128)} copy(f32[256,640]{1,0:T(8,128)} %get-tuple-element.9) | data formatting | bytes 1310720

commit v4 on v3

--- a/solution.py
+++ b/solution.py
@@ -11,6 +11,8 @@
 DS = 5120
 MESH = pl.DeviceIdType.MESH
 F32 = jnp.float32
+HALVES = ((0, 64), (64, 128))
+MOST, REST = (0, 112), (112, 128)
 BF16 = jnp.bfloat16
 
 
@@ -19,11 +21,11 @@
 
 
 def kernel(
-    t_ref, s_ref, loss_ref, grad_ref,
-    tb, sb, stage, rs, own, total, wn, wt, tst, red, redr, acc,
+    t_hbm, s_hbm, loss_ref, grad_ref, t_ref, s_ref,
+    tb, sb, stage, rs, own, total, wn, wt, tst, red, redr,
     t_ring, t_core, t_ring_out, t_core_out,
     s_ring, s_core, s_ring_out, s_core_out, x_out,
-    rs_in, rs_out, red_in, red_out, tr_in, tr_out, agn_in, agn_out, agt_in, agt_out,
+    rs_in, rs_out, red_in, red_out, tr_in, tr_out, agn_in, agn_out, agt_in, agt_out, load,
 ):
     tok = lax.axis_index("tok")
     feat = lax.axis_index("feat")
@@ -46,6 +48,10 @@
 
     swapped = core * 4 + y
 
+    loads = [pltpu.make_async_copy(a, b, load.at[i]) for i, (a, b) in enumerate(((t_hbm, t_ref), (s_hbm, s_ref)))]
+    for copy in loads:
+        copy.start()
+
     barrier = pltpu.get_barrier_semaphore()
 
     def greet(device):
@@ -56,6 +62,8 @@
     for device in (z_down, z_up, x_other, sibling):
         greet(device)
     pl.semaphore_wait(barrier, 11)
+    for copy in loads:
+        copy.wait()
 
     def send(src, dst, out_sem, in_sem, device):
         pltpu.make_async_remote_copy(
@@ -164,9 +172,9 @@
                 relay(kind, s, h, (0,))
             for h in range(2):
                 relay(kind, s, h, (1,) if early else (0, 1))
+                partials(kind, s, j, h)
                 if kind is T and s == 4 and h == 1:
                     pass_on(S, 4)
-                partials(kind, s, j, h)
             if kind is S and s:
                 step_sums(s - 1)
     step_sums(4)
@@ -181,8 +189,6 @@
     for g, peers in enumerate(groups):
         for i, device in enumerate(peers):
             send(red.at[g], redr.at[g, i], red_out.at[g], red_in.at[g], device)
-        for h in range(2):
-            relay(S, 5 + g, h)
         wait(redr.at[g], red_in.at[g])
         v = red[g]
         for i in range(15):
@@ -228,40 +234,44 @@
         buf, place, out, into = group
         ref = buf.at[place(f)]
         if part is not None:
-            ref = ref.at[part * 64 : (part + 1) * 64]
+            ref = ref.at[part[0] : part[1]]
         send(ref, ref, out.at[0], into.at[i], (tok, to))
 
     def got(group, f, part, i):
         buf, place, out, into = group
         ref = buf.at[place(f)]
         if part is not None:
-            ref = ref.at[part * 64 : (part + 1) * 64]
+            ref = ref.at[part[0] : part[1]]
         wait(ref, into.at[i])
 
     def first(group):
+        give(group, feat, None, across(feat), 2)
         give(group, feat, None, up, 0)
         give(group, feat, None, down, 1)
-        give(group, feat, None, across(feat), 2)
 
     def second(group):
         got(group, down, None, 0)
-        give(group, down, 0, up, 3)
+        give(group, down, HALVES[0], up, 3)
+        give(group, down, REST, across(feat), 9)
         got(group, up, None, 1)
-        give(group, up, 1, down, 4)
+        give(group, up, HALVES[1], down, 4)
+        give(group, up, REST, across(feat), 10)
         got(group, across(feat), None, 2)
-        give(group, across(feat), None, up, 5)
-        give(group, across(feat), None, down, 6)
+        give(group, across(feat), MOST, up, 5)
+        give(group, across(feat), MOST, down, 6)
 
     def third(group):
-        for part in range(2):
-            got(group, far, part, 3 + part)
-            give(group, far, part, across(feat), 7 + part)
+        for i, part in enumerate(HALVES):
+            got(group, far, part, 3 + i)
+            give(group, far, part, across(feat), 7 + i)
 
     def fourth(group):
-        got(group, across(down), None, 5)
-        got(group, across(up), None, 6)
-        for part in range(2):
-            got(group, across(far), part, 7 + part)
+        got(group, across(down), MOST, 5)
+        got(group, across(down), REST, 9)
+        got(group, across(up), MOST, 6)
+        got(group, across(up), REST, 10)
+        for i, part in enumerate(HALVES):
+            got(group, across(far), part, 7 + i)
 
     def product(buf, plane, lo, hi):
         @pl.loop(0, 2)
@@ -269,18 +279,22 @@
             a = 2 * plane + p
             depth = (hi - lo) * 256
             w = buf[pl.ds(2 * a, 2)].reshape(256, depth)
-            acc[...] += jnp.dot(w, sb[a, lo:hi].reshape(depth, DS // 8), preferred_element_type=F32)
+            grad_ref[...] += jnp.dot(w, sb[a, lo:hi].reshape(depth, DS // 8), preferred_element_type=F32)
 
     first(N)
     wait(wt.at[feat], tr_in.at[0])
     first(R)
+    for h in range(2):
+        relay(S, 5, h)
     second(N)
+    second(R)
+    for h in range(2):
+        relay(S, 6, h)
+    third(N)
+    third(R)
     for h in range(2):
         relay(S, 7, h)
-    second(R)
-    third(N)
-    third(R)
-    acc[...] = jnp.zeros_like(acc)
+    grad_ref[...] = jnp.zeros_like(grad_ref)
     product(wn, xh, 0, 5)
     for k in (5, 6, 7):
         for h in range(2):
@@ -290,8 +304,6 @@
     product(wn, 1 - xh, 0, 5)
     fourth(R)
     product(wt, 1 - xh, 5, 8)
-
-    grad_ref[...] = (2.0 * TOKENS * DS) * acc[...]
 
     for kind, index in ((S, 0), (T, 1)):
         src, buf, ring, cores, ring_out, core_out, last = kind
@@ -316,9 +328,11 @@
     loss, grad = pl.pallas_call(
         kernel,
         out_shape=(jax.ShapeDtypeStruct((1, 1), F32), jax.ShapeDtypeStruct((rows, ds), F32)),
-        in_specs=[pl.BlockSpec(memory_space=pltpu.VMEM)] * 2,
+        in_specs=[pl.BlockSpec(memory_space=pl.ANY)] * 2,
         out_specs=[pl.BlockSpec(memory_space=pltpu.VMEM)] * 2,
         scratch_shapes=[
+            pltpu.VMEM((rows, dt), BF16),
+            pltpu.VMEM((rows, ds), BF16),
             pltpu.VMEM((4, 5, 2, 128, dt), BF16),
             pltpu.VMEM((4, 8, 2, 128, ds), BF16),
             pltpu.VMEM((10, 8, 128, 256), BF16),
@@ -330,18 +344,17 @@
             pltpu.VMEM((6, 128, 128), BF16),
             pltpu.VMEM((3, 8, 128), F32),
             pltpu.VMEM((2, 15, 8, 128), F32),
-            pltpu.VMEM((rows, ds), F32),
             dma((5, 2, 2)), dma((5, 2)), dma((4,)), dma((5,)),
             dma((8, 2, 2)), dma((8, 2)), dma((7,)), dma((8,)), dma((2,)),
             dma((10,)), dma((10,)), dma((2,)), dma((2,)), dma((1,)), dma((1,)),
-            dma((9,)), dma((1,)), dma((9,)), dma((1,)),
+            dma((11,)), dma((1,)), dma((11,)), dma((1,)), dma((2,)),
         ],
         compiler_params=pltpu.CompilerParams(
             collective_id=0, has_side_effects=True, vmem_limit_bytes=60 * 2**20
         ),
         cost_estimate=pl.CostEstimate(flops=7 * 10**9, bytes_accessed=2 * 10**6, transcendentals=0),
     )(teacher, student)
-    return loss.reshape(()), grad
+    return loss.reshape(()), (2.0 * TOKENS * DS) * grad
 
 
 def solution(mesh):

time: 157 us -> 150 us (0.955); the launches traced: 154 us -> 150 us
  Pallas kernels: 150 us -> 145 us
  other arithmetic: 0 us -> 1.97 us
  local copies, waits for them, and re-layouts: 1.97 us -> 0 us
    pallas_call x1, Pallas kernels: 150 us -> 145 us  [local(): pl.pallas_call(kernel, out_shape=(jax.ShapeDtypeStruct((1, 1), F32), jax....]
    mul x0 -> x1, other arithmetic: none -> 1.97 us  [local(): return (loss.reshape(()), 2.0 * TOKENS * DS * grad)]
    unnamed x1 -> x0, local copies, waits for them, and re-layouts: 1.97 us -> none
where the time goes in v4:
time: 150 us
  Pallas kernels  145 us (97%)
  between operations  2.39 us (2%)
  other arithmetic  1.97 us (1%)
    pallas_call x1, Pallas kernels, local(): pl.pallas_call(kernel, out_shape=(jax.ShapeDtypeStruct((1, 1), F32), jax....  145 us

profile of v4, /device:TPU:1, one launch (start us, length us, event | category | flops | bytes accessed | tf_op | source)
XLA Modules:
  0.0 149.7 jit_solution(18136751591111098253)
XLA Ops:
  0.6 145.3 %shard_map.41 = (f32[1,1]{1,0:T(1,128)}, f32[256,640]{1,0:T(8,128)}) custom-call(bf16[256,1024]{1,0:T(8,128)(2,1)} %t_hbm.1, bf16[256,640]{1,0:T(8,128)(2,1)} %s_hbm.1), custom_call_target="tpu_custom_call" | custom-call | flops 7000000000 | bytes 2000000 | tf_op jit(solution)/shard_map/pallas_call | solution.py:328
  145.9 2.0 %broadcast_multiply_fusion = f32[256,640]{1,0:T(8,128)} fusion(f32[256,640]{1,0:T(8,128)} %get-tuple-element.5), kind=kLoop, calls=%fused_computation | loop fusion | flops 163840 | bytes 1310720 | tf_op jit(solution)/shard_map/mul | solution.py:357

commit v5 on v4

--- a/solution.py
+++ b/solution.py
@@ -89,11 +89,11 @@
             send(rows, buf.at[a, 0, 0], core_out.at[0], cores.at[0, h], sibling)
             buf[a, 0, 0] = src[h * 128 : (h + 1) * 128]
 
-    def relay(kind, k, h, sides=(0, 1)):
+    def relay(kind, k, h):
         src, buf, ring, cores, ring_out, core_out, last = kind
         here, there = slot(k), slot(k + 1)
         a = 2 * core + h
-        for side in sides if k else (1,):
+        for side in (0, 1) if k else (1,):
             block = buf.at[a, here, side]
             wait(block, ring.at[here, side, h])
             send(block, block, core_out.at[here], cores.at[here, h], sibling)
@@ -167,14 +167,15 @@
     red[0] = jnp.zeros((8, 128), F32)
     for s in range(5):
         for kind, j in ((S, 5 + s), (T, s)):
-            early = False
-            for h in range(2) if early else ():
-                relay(kind, s, h, (0,))
+            late = kind is T and s == 4
             for h in range(2):
-                relay(kind, s, h, (1,) if early else (0, 1))
+                relay(kind, s, h)
+                if late:
+                    partials(kind, s, j, h)
+            for h in () if late else range(2):
                 partials(kind, s, j, h)
-                if kind is T and s == 4 and h == 1:
-                    pass_on(S, 4)
+            if late:
+                pass_on(S, 4)
             if kind is S and s:
                 step_sums(s - 1)
     step_sums(4)

time: 150 us -> 149 us (level)
  Pallas kernels: 145 us -> 143 us
    pallas_call x1, Pallas kernels: 145 us -> 143 us  [local(): pl.pallas_call(kernel, out_shape=(jax.ShapeDtypeStruct((1, 1), F32), jax....]
where the time goes in v5:
time: 149 us; the launch traced here: 148 us
  Pallas kernels  143 us (96%)
  between operations  2.39 us (2%)
  other arithmetic  1.97 us (1%)
    pallas_call x1, Pallas kernels, local(): pl.pallas_call(kernel, out_shape=(jax.ShapeDtypeStruct((1, 1), F32), jax....  143 us

profile of v5, /device:TPU:1, one launch (start us, length us, event | category | flops | bytes accessed | tf_op | source)
XLA Modules:
  0.0 147.8 jit_solution(6481447913837312906)
XLA Ops:
  0.6 143.5 %shard_map.41 = (f32[1,1]{1,0:T(1,128)}, f32[256,640]{1,0:T(8,128)}) custom-call(bf16[256,1024]{1,0:T(8,128)(2,1)} %t_hbm.1, bf16[256,640]{1,0:T(8,128)(2,1)} %s_hbm.1), custom_call_target="tpu_custom_call" | custom-call | flops 7000000000 | bytes 2000000 | tf_op jit(solution)/shard_map/pallas_call | solution.py:329
  144.1 2.0 %broadcast_multiply_fusion = f32[256,640]{1,0:T(8,128)} fusion(f32[256,640]{1,0:T(8,128)} %get-tuple-element.5), kind=kLoop, calls=%fused_computation | loop fusion | flops 163840 | bytes 1310720 | tf_op jit(solution)/shard_map/mul | solution.py:358

commit v6 on v5

--- a/solution.py
+++ b/solution.py
@@ -170,12 +170,12 @@
             late = kind is T and s == 4
             for h in range(2):
                 relay(kind, s, h)
+                if late and h == 1:
+                    pass_on(S, 4)
                 if late:
                     partials(kind, s, j, h)
             for h in () if late else range(2):
                 partials(kind, s, j, h)
-            if late:
-                pass_on(S, 4)
             if kind is S and s:
                 step_sums(s - 1)
     step_sums(4)

time: 149 us -> 149 us (level)
  no operation moved by 1% of the time
where the time goes in v6:
time: 149 us; the launch traced here: 148 us
  Pallas kernels  144 us (97%)
  between operations  2.39 us (2%)
  other arithmetic  1.97 us (1%)
    pallas_call x1, Pallas kernels, local(): pl.pallas_call(kernel, out_shape=(jax.ShapeDtypeStruct((1, 1), F32), jax....  144 us

profile of v6, /device:TPU:1, one launch (start us, length us, event | category | flops | bytes accessed | tf_op | source)
XLA Modules:
  0.0 148.0 jit_solution(17914968493707290745)
XLA Ops:
  0.6 143.6 %shard_map.41 = (f32[1,1]{1,0:T(1,128)}, f32[256,640]{1,0:T(8,128)}) custom-call(bf16[256,1024]{1,0:T(8,128)(2,1)} %t_hbm.1, bf16[256,640]{1,0:T(8,128)(2,1)} %s_hbm.1), custom_call_target="tpu_custom_call" | custom-call | flops 7000000000 | bytes 2000000 | tf_op jit(solution)/shard_map/pallas_call | solution.py:329
  144.3 2.0 %broadcast_multiply_fusion = f32[256,640]{1,0:T(8,128)} fusion(f32[256,640]{1,0:T(8,128)} %get-tuple-element.5), kind=kLoop, calls=%fused_computation | loop fusion | flops 163840 | bytes 1310720 | tf_op jit(solution)/shard_map/mul | solution.py:358
